TPU v7x, 256 devices: a whole 4x4x8 slice. The times are simulated.
256 devices in a mesh: rows: 16 (over x, z_lo, core), cols: 16 (over z_hi, y).
Axes of the slice: x: 4, y: 4, z: 8 (z_hi: 4, z_lo: 2; z = z_hi * 2 + z_lo), core: 2. Of those that a mesh axis runs over, the one named last changes fastest.
Arguments:
- counts: int32 [32768, 16384], P('rows', 'cols'), may hold values from 0 to 256, as said below
- row_sums: int32 [32768], P('rows'), may hold values from 30000 to 999999
- col_sums: int32 [16384], P('cols'), may hold values from 30000 to 999999
- log_total: float32 [1], replicated, may hold values from 22 to 26
- row_emb: bfloat16 [32768, 256], P(('rows', 'cols')), may hold values from -1.5 to 1.5
- col_emb: bfloat16 [16384, 256], P(('cols', 'rows')), may hold values from -1.5 to 1.5
Outputs:
- row_grad: float32 [32768, 256], P(('rows', 'cols'))
- col_grad: float32 [16384, 256], P(('cols', 'rows'))
Inputs may be any that keep to these rules, and one draw needn't show every extreme that they name: `counts`: about five cells in fourteen are zero.
All inputs are finite; a program needn't handle non-finite values.
Results may differ from a plain program's by a relative error of at most 0.0013.
Values may be sent and summed in bfloat16 or wider, within the bound.
A program may use at most 64 MiB of HBM per device.

v0:
```python
import math

import jax
import jax.numpy as jnp
from jax import lax
from jax.sharding import PartitionSpec as P


def cell_grads(counts, scores, row_logs, col_logs, log_total, scale):
    count_f = counts.astype(jnp.float32)
    pmi = log_total - row_logs[:, None] - col_logs[None, :]
    conf = 0.1 + 0.25 * jnp.sqrt(count_f)
    fitted = conf * (scores - jnp.log(jnp.maximum(count_f, 1.0)) - pmi)
    hinge = jax.nn.sigmoid(scores - pmi)
    return (jnp.where(counts > 0, fitted, hinge) * scale).astype(jnp.bfloat16)


def tile_scores(row_block, col_whole):
    return lax.dot_general(
        row_block, col_whole, (((1,), (1,)), ((), ())), preferred_element_type=jnp.float32
    )


def shards(counts, row_sums, col_sums, log_total, row_emb, col_emb):
    n_cols = lax.axis_size("cols")
    tile = col_sums.shape[0]
    scale = 1.0 / math.sqrt(tile * n_cols)
    col_whole = lax.all_gather(col_emb, "rows", axis=0, tiled=True)
    col_logs = jnp.log(col_sums.astype(jnp.float32))
    row_logs = jnp.log(row_sums.astype(jnp.float32))
    rows_whole = lax.all_gather(row_emb, "cols", axis=0, tiled=True)
    grads = cell_grads(
        counts, tile_scores(rows_whole, col_whole), row_logs, col_logs, log_total[0], scale
    )
    row_grad = lax.psum_scatter(
        jnp.dot(grads, col_whole, preferred_element_type=jnp.float32),
        "cols",
        scatter_dimension=0,
        tiled=True,
    )
    total = lax.dot_general(
        grads, rows_whole, (((0,), (0,)), ((), ())), preferred_element_type=jnp.float32
    )
    col_grad = lax.psum_scatter(total, "rows", scatter_dimension=0, tiled=True)
    return (row_grad, col_grad)


def solution(mesh):
    in_specs = (
        P("rows", "cols"),
        P("rows"),
        P("cols"),
        P(),
        P(("rows", "cols"), None),
        P(("cols", "rows"), None),
    )
    out_specs = (P(("rows", "cols"), None), P(("cols", "rows"), None))
    return jax.shard_map(shards, mesh=mesh, in_specs=in_specs, out_specs=out_specs, check_vma=False)
```

profile of v0, /device:TPU:1, one launch (start us, length us, event | category | flops | bytes accessed | tf_op | source)
XLA Modules:
  0.0 243.0 jit_solution(6589093710645844163)
XLA Ops:
  7.2 0.0 all-gather.2.cloned.1.call-start
  7.2 0.7 all-gather.2.cloned.1.call-update
  7.9 0.0 reduce-scatter.5.cloned.1.call-start
  8.6 0.7 convert_log_fusion
  9.3 0.7 log_subtract_fusion
  10.0 24.0 %all_gather.7 = bf16[1024,256]{1,0:T(8,128)(2,1)S(1)} all-gather(bf16[64,256]{1,0:T(8,128)(2,1)} %param.11), channel_id=1, replica_groups=mesh['rows'=16,'cols'=16] {'rows'}, dimensions={0}, use_global_device_ids=true | all-gather | bytes 557056 | tf_op jit(solution)/shard_map/all_gather | solution.py:28
  34.0 32.6 %all-gather.2.cloned.1.call-done = bf16[2048,256]{1,0:T(8,128)(2,1)} async-done(((bf16[128,256]{1,0:T(8,128)(2,1)}), bf16[2048,256]{1,0:T(8,128)(2,1)}) %all-gather.2.cloned.1.call-update) | async-done | bytes 1048592 | tf_op jit(solution)/shard_map/all_gather | solution.py:31
  66.6 0.0 copy-start
  66.6 13.3 %fusion.3 = bf16[2048,1024]{1,0:T(8,128)(2,1)S(1)} fusion(s32[2048,1024]{1,0:T(8,128)} %param.6, f32[1024]{0:T(1024)S(1)} %convert_log_fusion, f32[2048]{0:T(1024)S(1)} %log_subtract_fusion, bf16[2048,256]{1,0:T(8,128)(2,1)} %all-gather.2.cloned.1.call-done, bf16[1024,256]{1,0:T(8,128)(2,1)S(1)} %all_gather.7), kind=kOutput, calls=%fused_computation.5 | convolution fusion | flops 1107296256 | bytes 14168064 | tf_op jit(solution)/shard_map/dot_general | solution.py:19
  79.9 0.0 copy-start.1
  79.9 1.9 copy-done.1
  81.9 0.0 copy-done
  81.9 2.3 fusion.9
  84.1 0.0 reduce-scatter.5.cloned.1.call-update
  84.2 0.0 reduce-scatter.3.cloned.1.call-start
  84.2 4.8 %fusion.8 = f32[2048,256]{1,0:T(8,128)} fusion(bf16[2048,1024]{1,0:T(8,128)(2,1)} %copy-done.1, bf16[1024,256]{1,0:T(8,128)(2,1)S(1)} %all_gather.7), kind=kOutput, calls=%fused_computation.12 | convolution fusion | flops 1073741824 | bytes 6815744 | tf_op jit(solution)/shard_map/dot_general | solution.py:36
  89.0 0.0 reduce-scatter.3.cloned.1.call-update
  89.0 54.5 %reduce-scatter.5.cloned.1.call-done = f32[64,256]{1,0:T(8,128)} async-done(((f32[1024,256]{1,0:T(8,128)}), f32[64,256]{1,0:T(8,128)}) %reduce-scatter.5.cloned.1.call-update) | async-done | bytes 65552 | tf_op jit(solution)/shard_map/reduce_scatter | solution.py:44
  143.5 93.0 %reduce-scatter.3.cloned.1.call-done = f32[128,256]{1,0:T(8,128)} async-done(((f32[2048,256]{1,0:T(8,128)}), f32[128,256]{1,0:T(8,128)}) %reduce-scatter.3.cloned.1.call-update) | async-done | bytes 131088 | tf_op jit(solution)/shard_map/reduce_scatter | solution.py:35
Async XLA Ops:
  7.2 59.5 %all-gather.2.cloned.1.call-start = ((), (), s32[]{:S(2)}) async-start(), calls=%async_computation.2 | async-start | bytes 1114112 | tf_op jit(solution)/shard_map/all_gather | solution.py:31
  7.9 135.6 %reduce-scatter.5.cloned.1.call-start = ((), (), s32[]{:S(2)}) async-start(), calls=%async_computation.4 | async-start | bytes 1114112 | tf_op jit(solution)/shard_map/reduce_scatter | solution.py:44
  66.6 15.2 %copy-start = (bf16[2048,256]{1,0:T(8,128)(2,1)S(1)}, bf16[2048,256]{1,0:T(8,128)(2,1)}, u32[]{:S(2)}) copy-start(bf16[2048,256]{1,0:T(8,128)(2,1)} %all-gather.2.cloned.1.call-done) | copy-start | bytes 3145732
  79.9 1.9 copy-start.1
  84.2 152.4 %reduce-scatter.3.cloned.1.call-start = ((), (), s32[]{:S(2)}) async-start(), calls=%async_computation.3 | async-start | bytes 2228224 | tf_op jit(solution)/shard_map/reduce_scatter | solution.py:35
Sparse Core Ops, SparseCore 0:
  10.4 56.1 all-gather.1
  84.3 59.1 reduce-scatter.4
  148.0 88.4 reduce-scatter.2
where the time goes:
time: 244 us; the launch traced here: 243 us
  waiting for transfers between devices  181 us (74%)
  blocking collectives  24 us (10%)
  matrix products  20.3 us (8%)
  between operations  14.4 us (6%)
    reduce_scatter x1, waiting for transfers between devices, shards(): lax.psum_scatter(jnp.dot(grads, col_whole, preferred_element_type=jnp.flo...  93 us
    reduce_scatter x1, waiting for transfers between devices, shards(): col_grad = lax.psum_scatter(total, 'rows', scatter_dimension=0, tiled=True)  54.5 us
    all_gather x1, waiting for transfers between devices, shards(): rows_whole = lax.all_gather(row_emb, 'cols', axis=0, tiled=True)  32.6 us
    all_gather x1, blocking collectives, shards(): col_whole = lax.all_gather(col_emb, 'rows', axis=0, tiled=True)  24 us
    dot_general x1, matrix products, tile_scores(): lax.dot_general(row_block, col_whole, (((1,), (1,)), ((), ())), preferred...  13.3 us
  transfers between devices with their start and end apart: 3, of which 3 were waited for; matrix products, arithmetic and copies ran while one was open for 3% of the time, Pallas kernels for 0%

commit v1 on v0

v1 whole, which is shorter than its diff:
```python
import math

import jax
import jax.numpy as jnp
from jax import lax
from jax.experimental import pallas as pl
from jax.experimental.pallas import tpu as pltpu
from jax.sharding import PartitionSpec as P

MESH = pl.DeviceIdType.MESH
D = 256
CHUNK = 128
PART = 64
SET = 4 * CHUNK
TILE = 4 * PART
LEVELS = 32000.0
STEPS = 8.0
ORDER = (1, 3, 2)


def encode(ref, value):
    rows = value.shape[0]
    top = jnp.max(jnp.abs(value), axis=0, keepdims=True)
    power = jnp.ceil(jnp.log(jnp.maximum(top, 1e-33)) * (STEPS / math.log(2.0)))
    inverse = jnp.exp(power * (-math.log(2.0) / STEPS)) * LEVELS
    ref[0:rows, :] = jnp.round(value * inverse).astype(jnp.int32).astype(jnp.int16)
    ref[rows : rows + 16, :] = (
        jnp.broadcast_to(power, (16, value.shape[1])).astype(jnp.int32).astype(jnp.int16)
    )


def decode(ref, rows):
    power = ref[rows : rows + 16, :].astype(jnp.int32).astype(jnp.float32)[0:1]
    scale = jnp.exp(power * (math.log(2.0) / STEPS)) * (1.0 / LEVELS)
    return ref[0:rows, :].astype(jnp.int32).astype(jnp.float32) * scale


def cell_grads(counts, scores, scale):
    at_least_one = jnp.maximum(counts.astype(jnp.float32), 1.0)
    root = at_least_one * lax.rsqrt(at_least_one)
    conf = (0.1 * scale) + (0.25 * scale) * root
    fitted = conf * (scores - jnp.log(at_least_one))
    hinge = (0.5 * scale) + (0.5 * scale) * jnp.tanh(0.5 * scores)
    return jnp.where(counts > 0, fitted, hinge).astype(jnp.bfloat16)


def kernel(
    scale,
    counts_hbm, row_sums_hbm, col_sums_hbm, log_total, row_emb, col_emb,
    row_out, col_out,
    counts, row_sums, col_sums, rows, cols, row_bias, col_bias,
    kept, row_total, col_total,
    y_out, y_in, z_out, z_in, c_out, c_in, x_out, x_in,
    local_sem, counts_sem,
    gz_send, gz_recv, gy_send, gy_recv, gx_send, gx_recv, gc_send, gc_recv,
    ry_send, ry_recv, rz_send, rz_recv, rc_send, rc_recv, rx_send, rx_recv,
):
    r, k = lax.axis_index("rows"), lax.axis_index("cols")
    x, zl, c = r // 4, (r // 2) % 2, r % 2
    zh, y = k // 4, k % 4

    def col_peer(dz, dy):
        return (r, lax.rem(zh + dz, 4) * 4 + lax.rem(y + dy, 4))

    def row_peer(dx, dl, dc):
        return (lax.rem(x + dx, 4) * 4 + lax.rem(zl + dl, 2) * 2 + lax.rem(c + dc, 2), k)

    def chunk_at(z, yy):
        return pl.ds(pl.multiple_of((z * 4 + yy) * CHUNK, CHUNK), CHUNK)

    def part_at(index):
        return pl.ds(pl.multiple_of(index * PART, PART), PART)

    def remote(src, dst, send, recv, to):
        return pltpu.make_async_remote_copy(
            src_ref=src, dst_ref=dst, send_sem=send, recv_sem=recv, device_id=to, device_id_type=MESH
        )

    same_core = [(dx, dl) for dx in range(4) for dl in range(2) if dx or dl]

    own_rows, own_cols = chunk_at(zh, y), part_at(r)
    local = [
        pltpu.make_async_copy(row_emb, rows.at[own_rows], local_sem.at[0]),
        pltpu.make_async_copy(col_emb, cols.at[own_cols], local_sem.at[1]),
        pltpu.make_async_copy(row_sums_hbm, row_sums, local_sem.at[2]),
        pltpu.make_async_copy(col_sums_hbm, col_sums, local_sem.at[3]),
    ]
    for copy in local:
        copy.start()
    barrier = pltpu.get_barrier_semaphore()
    peers = [col_peer(d, 0) for d in (1, 2, 3)] + [col_peer(0, d) for d in (1, 2, 3)]
    peers += [row_peer(dx, dl, 0) for dx, dl in same_core] + [row_peer(0, 0, 1)]
    for peer in peers:
        pl.semaphore_signal(barrier, inc=1, device_id=peer, device_id_type=MESH)
    counts_in = []
    for n in range(4):
        at = pl.ds(n * SET, SET)
        counts_in.append(pltpu.make_async_copy(counts_hbm.at[at], counts.at[at], counts_sem.at[n]))
        counts_in[-1].start()
    for copy in local:
        copy.wait()
    pl.semaphore_wait(barrier, len(peers))

    sends = []

    def go(copy):
        copy.start()
        sends.append(copy)
        return copy

    for d in ORDER:
        go(remote(rows.at[own_rows], rows.at[own_rows], gz_send.at[d], gz_recv.at[d], col_peer(d, 0)))
    for e in (1, 3, 2):
        go(remote(rows.at[own_rows], rows.at[own_rows], gy_send.at[0, e], gy_recv.at[0, e], col_peer(0, e)))
    for n, (dx, dl) in enumerate(same_core):
        go(remote(cols.at[own_cols], cols.at[own_cols], gx_send.at[n], gx_recv.at[n], row_peer(dx, dl, 0)))
    go(remote(cols.at[own_cols], cols.at[own_cols], gc_send.at[7], gc_recv.at[7], row_peer(0, 0, 1)))

    row_logs = jnp.log(row_sums[...].astype(jnp.float32)) - log_total[0]
    for n in range(16):
        square = jnp.broadcast_to(row_logs[n : n + 1, :], (CHUNK, CHUNK))
        row_bias[n * CHUNK : (n + 1) * CHUNK, :] = square.T
    col_logs = jnp.log(col_sums[...].astype(jnp.float32))
    for t in range(4):
        both = [jnp.broadcast_to(col_logs[2 * t + h : 2 * t + h + 1, :], (8, CHUNK)) for h in (0, 1)]
        col_bias[t] = jnp.concatenate(both, axis=1)
    col_total[...] = jnp.zeros_like(col_total)

    def forward_rows(d):
        z = lax.rem(zh + 4 - d, 4)
        at = chunk_at(z, y)
        remote(rows.at[at], rows.at[at], gz_send.at[d], gz_recv.at[d], col_peer(d, 0)).wait_recv()
        for e in (1, 3, 2):
            go(remote(rows.at[at], rows.at[at], gy_send.at[d, e], gy_recv.at[d, e], col_peer(0, e)))

    def forward_cols(n):
        dx, dl = same_core[n]
        origin = lax.rem(x + 4 - dx, 4) * 4 + lax.rem(zl + dl, 2) * 2 + c
        at = part_at(origin)
        remote(cols.at[at], cols.at[at], gx_send.at[n], gx_recv.at[n], row_peer(dx, dl, 0)).wait_recv()
        go(remote(cols.at[at], cols.at[at], gc_send.at[n], gc_recv.at[n], row_peer(0, 0, 1)))

    forward_rows(1)
    forward_rows(3)
    for n in range(7):
        forward_cols(n)
    forward_rows(2)
    for n in range(8):
        dx, dl = same_core[n] if n < 7 else (0, 0)
        origin = lax.rem(x + 4 - dx, 4) * 4 + lax.rem(zl + dl, 2) * 2 + (1 - c)
        at = part_at(origin)
        remote(cols.at[at], cols.at[at], gc_send.at[n], gc_recv.at[n], row_peer(0, 0, 1)).wait_recv()
    for copy in counts_in:
        copy.wait()

    def wait_set(d):
        z = lax.rem(zh + 4 - d, 4)
        for e in (1, 3, 2):
            at = chunk_at(z, lax.rem(y + 4 - e, 4))
            remote(rows.at[at], rows.at[at], gy_send.at[d, e], gy_recv.at[d, e], col_peer(0, e)).wait_recv()

    def grads_of(at, tile, width):
        col_at = pl.ds(pl.multiple_of(tile * TILE, TILE), width)
        some = cols[col_at, :]
        scores = lax.dot_general(
            rows[at, :], some, (((1,), (1,)), ((), ())), preferred_element_type=jnp.float32
        )
        bias = jnp.concatenate([row_bias[at, :]] * (width // CHUNK), axis=1)
        side = jnp.concatenate([col_bias[tile + n, 0:1, :] for n in range(width // TILE)], axis=1)
        return cell_grads(counts[at, col_at], scores + bias + side, scale), some, col_at

    def send_rows(d, total):
        for e in (2, 1, 3):
            encode(y_out.at[d, e - 1], total[pl.ds(pl.multiple_of(lax.rem(y + e, 4) * CHUNK, CHUNK), CHUNK), :])
            remote(y_out.at[d, e - 1], y_in.at[d, e - 1], ry_send.at[d, e], ry_recv.at[d, e], col_peer(0, e)).start()
        kept[d] = total[pl.ds(pl.multiple_of(y * CHUNK, CHUNK), CHUNK), :]

    def sum_rows(d):
        total = kept[d]
        for e in (1, 3, 2):
            remote(y_out.at[d, e - 1], y_in.at[d, e - 1], ry_send.at[d, e], ry_recv.at[d, e], col_peer(0, e)).wait_recv()
            total = total + decode(y_in.at[d, e - 1], CHUNK)
        return total

    def send_z(d):
        encode(z_out.at[d - 1], sum_rows(d))
        go(remote(z_out.at[d - 1], z_in.at[d - 1], rz_send.at[d], rz_recv.at[d], col_peer(4 - d, 0)))

    def one_set(step, _):
        d = lax.rem(1 + 2 * step - 3 * (step // 2), 4)
        z = lax.rem(zh + 4 - d, 4)
        wait_set(d)
        at = pl.ds(pl.multiple_of(z * SET, SET), SET)
        for tile in (0, 2):
            grads, some, col_at = grads_of(at, tile, 2 * TILE)
            part = jnp.dot(grads, some, preferred_element_type=jnp.float32)
            row_total[...] = part if tile == 0 else row_total[...] + part
            col_total[col_at, :] += lax.dot_general(
                grads, rows[at, :], (((0,), (0,)), ((), ())), preferred_element_type=jnp.float32
            )
        send_rows(d, row_total)
        return 0

    lax.fori_loop(0, 3, one_set, 0)
    send_z(1)

    wait_set(0)
    at = pl.ds(pl.multiple_of(zh * SET, SET), SET)
    for n in range(4):
        tile = lax.rem(x + 1 + n, 4)
        grads, some, col_at = grads_of(at, tile, TILE)
        part = jnp.dot(grads, some, preferred_element_type=jnp.float32)
        row_total[...] = part if n == 0 else row_total[...] + part
        col_total[col_at, :] += lax.dot_general(
            grads, rows[at, :], (((0,), (0,)), ((), ())), preferred_element_type=jnp.float32
        )
        theirs = [col_total[part_at(tile * 4 + 2 * h + 1 - c), :] for h in (0, 1)]
        encode(c_out.at[n], jnp.concatenate(theirs, axis=0))
        go(remote(c_out.at[n], c_in.at[n], rc_send.at[n], rc_recv.at[n], row_peer(0, 0, 1)))
    send_rows(0, row_total)


    own_cols_sum = None
    for n in range(4):
        tile = lax.rem(x + 1 + n, 4)
        remote(c_out.at[n], c_in.at[n], rc_send.at[n], rc_recv.at[n], row_peer(0, 0, 1)).wait_recv()
        mine = [col_total[part_at(tile * 4 + 2 * h + c), :] for h in (0, 1)]
        both = decode(c_in.at[n], 2 * PART) + jnp.concatenate(mine, axis=0)
        here = jnp.where(zl == 0, both[0:PART], both[PART:])
        there = jnp.where(zl == 0, both[PART:], both[0:PART])
        slot = 2 * n
        if n < 3:
            encode(x_out.at[slot + 1], here)
            go(remote(x_out.at[slot + 1], x_in.at[slot + 1], rx_send.at[slot + 1], rx_recv.at[slot + 1], row_peer(n + 1, 0, 0)))
        else:
            own_cols_sum = here
        encode(x_out.at[slot], there)
        go(remote(x_out.at[slot], x_in.at[slot], rx_send.at[slot], rx_recv.at[slot], row_peer((n + 1) % 4, 1, 0)))

    send_z(3)
    send_z(2)
    row_sum = sum_rows(0)
    for slot in range(7):
        n, dl = slot // 2, 1 - slot % 2
        remote(x_out.at[slot], x_in.at[slot], rx_send.at[slot], rx_recv.at[slot], row_peer((n + 1) % 4, dl, 0)).wait_recv()
        own_cols_sum = own_cols_sum + decode(x_in.at[slot], PART)
    col_out[...] = own_cols_sum
    for d in ORDER:
        remote(z_out.at[d - 1], z_in.at[d - 1], rz_send.at[d], rz_recv.at[d], col_peer(4 - d, 0)).wait_recv()
        row_sum = row_sum + decode(z_in.at[d - 1], CHUNK)
    row_out[...] = row_sum

    for copy in sends:
        copy.wait_send()
    for d in range(4):
        for e in (1, 2, 3):
            remote(y_out.at[d, e - 1], y_in.at[d, e - 1], ry_send.at[d, e], ry_recv.at[d, e], col_peer(0, e)).wait_send()


def shards(counts, row_sums, col_sums, log_total, row_emb, col_emb):
    n_cols = lax.axis_size("cols")
    scale = 1.0 / math.sqrt(col_sums.shape[0] * n_cols)
    dma = pltpu.SemaphoreType.DMA

    def body(*refs):
        kernel(scale, *refs)

    anywhere = pl.BlockSpec(memory_space=pl.ANY)
    vmem = pl.BlockSpec(memory_space=pltpu.VMEM)
    message = (CHUNK + 16, D)
    return pl.pallas_call(
        body,
        name="swivel",
        out_shape=(
            jax.ShapeDtypeStruct((CHUNK, D), jnp.float32),
            jax.ShapeDtypeStruct((PART, D), jnp.float32),
        ),
        in_specs=[anywhere] * 3 + [pl.BlockSpec(memory_space=pltpu.SMEM)] + [anywhere] * 2,
        out_specs=(vmem, vmem),
        scratch_shapes=[
            pltpu.VMEM(counts.shape, jnp.int32),
            pltpu.VMEM((16, CHUNK), jnp.int32),
            pltpu.VMEM((8, CHUNK), jnp.int32),
            pltpu.VMEM((16 * CHUNK, D), jnp.bfloat16),
            pltpu.VMEM((16 * PART, D), jnp.bfloat16),
            pltpu.VMEM((16 * CHUNK, CHUNK), jnp.float32),
            pltpu.VMEM((4, 8, TILE), jnp.float32),
            pltpu.VMEM((4, CHUNK, D), jnp.float32),
            pltpu.VMEM((SET, D), jnp.float32),
            pltpu.VMEM((16 * PART, D), jnp.float32),
            pltpu.VMEM((4, 3) + message, jnp.int16),
            pltpu.VMEM((4, 3) + message, jnp.int16),
            pltpu.VMEM((3,) + message, jnp.int16),
            pltpu.VMEM((3,) + message, jnp.int16),
            pltpu.VMEM((4,) + message, jnp.int16),
            pltpu.VMEM((4,) + message, jnp.int16),
            pltpu.VMEM((7, PART + 16, D), jnp.int16),
            pltpu.VMEM((7, PART + 16, D), jnp.int16),
            dma((4,)),
            dma((4,)),
            dma((4,)), dma((4,)),
            dma((4, 4)), dma((4, 4)),
            dma((7,)), dma((7,)),
            dma((8,)), dma((8,)),
            dma((4, 4)), dma((4, 4)),
            dma((4,)), dma((4,)),
            dma((4,)), dma((4,)),
            dma((7,)), dma((7,)),
        ],
        compiler_params=pltpu.CompilerParams(
            collective_id=0, has_side_effects=True, vmem_limit_bytes=48 << 20
        ),
        cost_estimate=pl.CostEstimate(
            flops=6 * 2048 * 1024 * 256, bytes_accessed=9 << 20, transcendentals=3 * 2048 * 1024
        ),
    )(counts, row_sums.reshape(16, CHUNK), col_sums.reshape(8, CHUNK), log_total, row_emb, col_emb)


def solution(mesh):
    in_specs = (
        P("rows", "cols"),
        P("rows"),
        P("cols"),
        P(),
        P(("rows", "cols"), None),
        P(("cols", "rows"), None),
    )
    out_specs = (P(("rows", "cols"), None), P(("cols", "rows"), None))
    return jax.shard_map(shards, mesh=mesh, in_specs=in_specs, out_specs=out_specs, check_vma=False)
```

time: 244 us -> 52.7 us (0.22)
  waiting for transfers between devices: 181 us -> 0 us
  Pallas kernels: 0 us -> 46.9 us
  blocking collectives: 24 us -> 0 us
  matrix products: 20.3 us -> 0 us
  between operations: 14.4 us -> 1.3 us
    reduce_scatter x2 -> x0, waiting for transfers between devices: 148 us -> none  [the longest x1 93 us: shards(): lax.psum_scatter(jnp.dot(grads, col_whole, preferred_element_type=jnp.flo...]
    pallas_call x0 -> x1, Pallas kernels: none -> 46.9 us  [shards(): pl.pallas_call(body, name='swivel', out_shape=(jax.ShapeDtypeStruct((CHUN...]
    all_gather x1 -> x0, waiting for transfers between devices: 32.6 us -> none  [shards(): rows_whole = lax.all_gather(row_emb, 'cols', axis=0, tiled=True)]
    all_gather x1 -> x0, blocking collectives: 24 us -> none  [shards(): col_whole = lax.all_gather(col_emb, 'rows', axis=0, tiled=True)]
    dot_general x3 -> x0, matrix products: 20.3 us -> none  [the longest x1 13.3 us: tile_scores(): lax.dot_general(row_block, col_whole, (((1,), (1,)), ((), ())), preferred...]
  transfers between devices with their start and end apart: 3 -> 0, of which waited for: 3 -> 0; matrix products, arithmetic and copies ran while one was open for 3% -> 0% of each run, Pallas kernels for 0% -> 0%
where the time goes in v1:
time: 52.7 us; the launch traced here: 52.4 us
  Pallas kernels  46.9 us (89%)
  local copies, waits for them, and re-layouts  4.26 us (8%)
  between operations  1.3 us (2%)
    pallas_call x1, Pallas kernels, shards(): pl.pallas_call(body, name='swivel', out_shape=(jax.ShapeDtypeStruct((CHUN...  46.9 us
    unnamed x10, local copies, waits for them, and re-layouts  4.26 us

profile of v1, /device:TPU:1, one launch (start us, length us, event | category | flops | bytes accessed | tf_op | source)
XLA Modules:
  0.0 52.4 jit_solution(2221930842639261670)
XLA Ops:
  1.3 0.0 copy-start
  1.3 0.8 %copy-done = bf16[128,256]{1,0:T(8,128)(2,1)S(1)} copy-done((bf16[128,256]{1,0:T(8,128)(2,1)S(1)}, bf16[128,256]{1,0:T(8,128)(2,1)}, u32[]{:S(2)}) %copy-start) | copy-done | bytes 65560
  2.1 0.0 copy-start.1
  2.1 0.8 %copy-done.1 = bf16[64,256]{1,0:T(8,128)(2,1)S(1)} copy-done((bf16[64,256]{1,0:T(8,128)(2,1)S(1)}, bf16[64,256]{1,0:T(8,128)(2,1)}, u32[]{:S(2)}) %copy-start.1) | copy-done | bytes 32792
  2.9 0.0 copy-start.2
  2.9 0.7 %copy-done.2 = s32[2048]{0:T(1024)S(1)} copy-done((s32[2048]{0:T(1024)S(1)}, s32[2048]{0:T(1024)}, u32[]{:S(2)}) %copy-start.2) | copy-done | bytes 8216
  3.6 0.0 copy-start.3
  3.6 0.7 %copy-done.3 = s32[1024]{0:T(1024)S(1)} copy-done((s32[1024]{0:T(1024)S(1)}, s32[1024]{0:T(1024)}, u32[]{:S(2)}) %copy-start.3) | copy-done | bytes 4120
  4.3 46.9 %swivel.1 = (f32[128,256]{1,0:T(8,128)S(1)}, f32[64,256]{1,0:T(8,128)S(1)}) custom-call(s32[2048,1024]{1,0:T(8,128)} %refs_0_.1, s32[16,128]{1,0:T(8,128)S(1)} %bitcast.2, s32[8,128]{1,0:T(8,128)S(1)} %bitcast.3, f32[1]{0:T(128)S(6)} %copy.10.refs_3_, bf16[128,256]{1,0:T(8,128)(2,1)S(1)} %copy-done, bf16[64,256]{1,0:T(8,128)(2,1)S(1)} %copy-done.1), custom_call_target="tpu_custom_call" | custom-call | flops 3221225472 | bytes 9437184 | tf_op jit(solution)/shard_map/swivel/pallas_call | solution.py:271
  51.2 0.7 %copy.11 = f32[128,256]{1,0:T(8,128)} copy(f32[128,256]{1,0:T(8,128)S(1)} %get-tuple-element.4) | data formatting | bytes 262144
  51.8 0.6 %copy.12 = f32[64,256]{1,0:T(8,128)} copy(f32[64,256]{1,0:T(8,128)S(1)} %get-tuple-element.5) | data formatting | bytes 131072
Async XLA Ops:
  1.3 0.8 %copy-start = (bf16[128,256]{1,0:T(8,128)(2,1)S(1)}, bf16[128,256]{1,0:T(8,128)(2,1)}, u32[]{:S(2)}) copy-start(bf16[128,256]{1,0:T(8,128)(2,1)} %refs_4_.1) | copy-start | bytes 196612
  2.1 0.8 %copy-start.1 = (bf16[64,256]{1,0:T(8,128)(2,1)S(1)}, bf16[64,256]{1,0:T(8,128)(2,1)}, u32[]{:S(2)}) copy-start(bf16[64,256]{1,0:T(8,128)(2,1)} %refs_5_.1) | copy-start | bytes 98308
  2.9 0.7 %copy-start.2 = (s32[2048]{0:T(1024)S(1)}, s32[2048]{0:T(1024)}, u32[]{:S(2)}) copy-start(s32[2048]{0:T(1024)} %param.7) | copy-start | bytes 24580
  3.6 0.7 %copy-start.3 = (s32[1024]{0:T(1024)S(1)}, s32[1024]{0:T(1024)}, u32[]{:S(2)}) copy-start(s32[1024]{0:T(1024)} %param.8) | copy-start | bytes 12292

commit v2 on v1

v2 whole, which is shorter than its diff:
```python
import math

import jax
import jax.numpy as jnp
from jax import lax
from jax.experimental import pallas as pl
from jax.experimental.pallas import tpu as pltpu
from jax.sharding import PartitionSpec as P

MESH = pl.DeviceIdType.MESH
D = 256
CHUNK = 128
PART = 64
SET = 4 * CHUNK
TILE = 4 * PART
LEVELS = 32000.0
STEPS = 8.0
COLUMN_ORDER = (0, 1, 5, 3, 2, 6, 4)
SETS = (1, 2, 3)


def encode(ref, value):
    rows = value.shape[0]
    top = jnp.max(jnp.abs(value), axis=0, keepdims=True)
    power = jnp.ceil(jnp.log(jnp.maximum(top, 1e-33)) * (STEPS / math.log(2.0)))
    inverse = jnp.exp(power * (-math.log(2.0) / STEPS)) * LEVELS
    ref[0:rows, :] = jnp.round(value * inverse).astype(jnp.int32).astype(jnp.int16)
    ref[rows : rows + 16, :] = (
        jnp.broadcast_to(power, (16, value.shape[1])).astype(jnp.int32).astype(jnp.int16)
    )


def decode(ref, rows):
    power = ref[rows : rows + 16, :].astype(jnp.int32).astype(jnp.float32)[0:1]
    scale = jnp.exp(power * (math.log(2.0) / STEPS)) * (1.0 / LEVELS)
    return ref[0:rows, :].astype(jnp.int32).astype(jnp.float32) * scale


def cell_grads(counts, scores, scale):
    at_least_one = jnp.maximum(counts.astype(jnp.float32), 1.0)
    root = at_least_one * lax.rsqrt(at_least_one)
    conf = (0.1 * scale) + (0.25 * scale) * root
    fitted = conf * (scores - jnp.log(at_least_one))
    hinge = (0.5 * scale) + (0.5 * scale) * jnp.tanh(0.5 * scores)
    return jnp.where(counts > 0, fitted, hinge).astype(jnp.bfloat16)


def kernel(
    scale,
    counts_hbm, row_sums_hbm, col_sums_hbm, log_total, row_emb, col_emb,
    row_out, col_out,
    counts, row_sums, col_sums, rows, cols, row_bias, col_bias,
    kept, far, row_total, col_total,
    y_out, y_in, b_in, z_out, z_in, c_out, c_in, x_out, x_in, l_out, l_in,
    local_sem, counts_sem,
    gz_send, gz_recv, gy_send, gy_recv, gx_send, gx_recv, gc_send, gc_recv,
    ry_send, ry_recv, rb_send, rb_recv, rz_send, rz_recv, rc_send, rc_recv, rx_send, rx_recv, rl_send, rl_recv,
):
    r, k = lax.axis_index("rows"), lax.axis_index("cols")
    x, zl, c = r // 4, (r // 2) % 2, r % 2
    zh, y = k // 4, k % 4

    def col_peer(dz, dy):
        return (r, lax.rem(zh + dz, 4) * 4 + lax.rem(y + dy, 4))

    def row_peer(dx, dl, dc):
        return (lax.rem(x + dx, 4) * 4 + lax.rem(zl + dl, 2) * 2 + lax.rem(c + dc, 2), k)

    def chunk_at(z, yy):
        return pl.ds(pl.multiple_of((z * 4 + yy) * CHUNK, CHUNK), CHUNK)

    def part_at(index):
        return pl.ds(pl.multiple_of(index * PART, PART), PART)

    def remote(src, dst, send, recv, to):
        return pltpu.make_async_remote_copy(
            src_ref=src, dst_ref=dst, send_sem=send, recv_sem=recv, device_id=to, device_id_type=MESH
        )

    same_core = [(dx, dl) for dx in range(4) for dl in range(2) if dx or dl]

    own_rows, own_cols = chunk_at(zh, y), part_at(r)
    local = [
        pltpu.make_async_copy(row_emb, rows.at[own_rows], local_sem.at[0]),
        pltpu.make_async_copy(col_emb, cols.at[own_cols], local_sem.at[1]),
        pltpu.make_async_copy(row_sums_hbm, row_sums, local_sem.at[2]),
        pltpu.make_async_copy(col_sums_hbm, col_sums, local_sem.at[3]),
    ]
    for copy in local:
        copy.start()
    barrier = pltpu.get_barrier_semaphore()
    peers = [col_peer(d, 0) for d in (1, 2, 3)] + [col_peer(0, d) for d in (1, 2, 3)]
    peers += [row_peer(dx, dl, 0) for dx, dl in same_core] + [row_peer(0, 0, 1)]
    for peer in peers:
        pl.semaphore_signal(barrier, inc=1, device_id=peer, device_id_type=MESH)
    counts_in = []
    for n in range(4):
        at = pl.ds(n * SET, SET)
        counts_in.append(pltpu.make_async_copy(counts_hbm.at[at], counts.at[at], counts_sem.at[n]))
        counts_in[-1].start()
    for copy in local:
        copy.wait()
    pl.semaphore_wait(barrier, len(peers))

    sends = []

    def go(copy):
        copy.start()
        sends.append(copy)
        return copy

    def z_gather(d):
        at = chunk_at(lax.rem(zh + 4 - d, 4), y)
        return remote(rows.at[at], rows.at[at], gz_send.at[d], gz_recv.at[d], col_peer(d, 0))

    def send_cols(dx, dl):
        at, n = part_at(x * 4 + lax.rem(zl + dl, 2) * 2 + c), 2 * dx + dl - 1
        go(remote(cols.at[at], cols.at[at], gx_send.at[n], gx_recv.at[n], row_peer(dx, 0, 0)))

    def send_own_rows(d):
        go(remote(rows.at[own_rows], rows.at[own_rows], gz_send.at[d], gz_recv.at[d], col_peer(d, 0)))

    send_own_rows(1)
    send_own_rows(3)
    go(remote(cols.at[own_cols], cols.at[own_cols], gc_send.at[7], gc_recv.at[7], row_peer(0, 0, 1)))
    go(remote(cols.at[own_cols], cols.at[own_cols], gx_send.at[0], gx_recv.at[0], row_peer(0, 1, 0)))
    for dx in (1, 3, 2):
        send_cols(dx, 0)
    for e in (1, 3, 2):
        go(remote(rows.at[own_rows], rows.at[own_rows], gy_send.at[0, e], gy_recv.at[0, e], col_peer(0, e)))
    send_own_rows(2)

    row_logs = jnp.log(row_sums[...].astype(jnp.float32)) - log_total[0]
    for n in range(16):
        square = jnp.broadcast_to(row_logs[n : n + 1, :], (CHUNK, CHUNK))
        row_bias[n * CHUNK : (n + 1) * CHUNK, :] = square.T
    col_logs = jnp.log(col_sums[...].astype(jnp.float32))
    for t in range(4):
        both = [jnp.broadcast_to(col_logs[2 * t + h : 2 * t + h + 1, :], (8, CHUNK)) for h in (0, 1)]
        col_bias[t] = jnp.concatenate(both, axis=1)

    def forward_rows(d):
        at = chunk_at(lax.rem(zh + 4 - d, 4), y)
        z_gather(d).wait_recv()
        for e in (1, 3, 2):
            go(remote(rows.at[at], rows.at[at], gy_send.at[d, e], gy_recv.at[d, e], col_peer(0, e)))

    def y_gather(d, e):
        at = chunk_at(lax.rem(zh + 4 - d, 4), lax.rem(y + 4 - e, 4))
        return remote(rows.at[at], rows.at[at], gy_send.at[d, e], gy_recv.at[d, e], col_peer(0, e))

    def origin(dx, dl, core):
        return part_at(lax.rem(x + 4 - dx, 4) * 4 + lax.rem(zl + dl, 2) * 2 + core)

    def forward_cols(n):
        dx, dl = same_core[n]
        at = origin(dx, dl, c)
        remote(cols.at[at], cols.at[at], gx_send.at[n], gx_recv.at[n], row_peer(dx, dl, 0)).wait_recv()
        go(remote(cols.at[at], cols.at[at], gc_send.at[n], gc_recv.at[n], row_peer(0, 0, 1)))
        if n == 0:
            for peer in (1, 3, 2):
                send_cols(peer, 1)

    def wait_cols(dx):
        for dl in (0, 1):
            n = lax.rem(2 * dx + dl + 7, 8)
            at = origin(dx, dl, 1 - c)
            remote(cols.at[at], cols.at[at], gc_send.at[n], gc_recv.at[n], row_peer(0, 0, 1)).wait_recv()

    def wait_set(d):
        for e in (1, 3, 2):
            y_gather(d, e).wait_recv()

    def grads_of(at, tile, width):
        col_at = pl.ds(pl.multiple_of(tile * TILE, TILE), width)
        some = cols[col_at, :]
        scores = lax.dot_general(
            rows[at, :], some, (((1,), (1,)), ((), ())), preferred_element_type=jnp.float32
        )
        bias = jnp.concatenate([row_bias[at, :]] * (width // CHUNK), axis=1)
        side = jnp.concatenate([col_bias[tile + n, 0:1, :] for n in range(width // TILE)], axis=1)
        return cell_grads(counts[at, col_at], scores + bias + side, scale), some, col_at

    def tile_step(at, tile, width, first_rows, first_cols):
        grads, some, col_at = grads_of(at, tile, width)
        part = jnp.dot(grads, some, preferred_element_type=jnp.float32)
        row_total[...] = part if first_rows else row_total[...] + part
        part = lax.dot_general(
            grads, rows[at, :], (((0,), (0,)), ((), ())), preferred_element_type=jnp.float32
        )
        col_total[col_at, :] = part if first_cols else col_total[col_at, :] + part

    def set_at(d):
        return pl.ds(pl.multiple_of(lax.rem(zh + 4 - d, 4) * SET, SET), SET)

    def y_message(d, e):
        return remote(
            y_out.at[d, e - 1], y_in.at[d, e - 1], ry_send.at[d, e], ry_recv.at[d, e], col_peer(0, e)
        )

    def far_message(d):
        n = d // 2
        return remote(y_out.at[d, 1], b_in.at[n], rb_send.at[n], rb_recv.at[n], col_peer(4 - d, 0))

    def z_message(d):
        return remote(z_out.at[d - 1], z_in.at[d - 1], rz_send.at[d], rz_recv.at[d], col_peer(4 - d, 0))

    def peer_rows(e):
        return row_total[pl.ds(pl.multiple_of(lax.rem(y + e, 4) * CHUNK, CHUNK), CHUNK), :]

    def encode_rows(d):
        if d == 0:
            far[...] = peer_rows(2)
        else:
            encode(y_out.at[d, 1], peer_rows(2))
        encode(y_out.at[d, 0], peer_rows(1))
        encode(y_out.at[d, 2], peer_rows(3))
        kept[d] = peer_rows(0)

    def send_rows(d):
        if d % 2:
            far_message(d).start()
        elif d:
            y_message(d, 2).start()
        y_message(d, 1).start()
        y_message(d, 3).start()

    def send_far():
        for d in (1, 3):
            far_message(d).wait_recv()
        encode(y_out.at[0, 1], far[...] + decode(b_in.at[0], CHUNK) + decode(b_in.at[1], CHUNK))
        y_message(0, 2).start()

    def sum_rows(d):
        hops = (1, 3) if d % 2 else (1, 3, 2)
        total = kept[d]
        for e in hops:
            y_message(d, e).wait_recv()
        for e in hops:
            total = total + decode(y_in.at[d, e - 1], CHUNK)
        return total

    def send_z(d):
        encode(z_out.at[d - 1], sum_rows(d))
        z_message(d).start()

    odd, pair = x % 2, x // 2
    forward_cols(0)
    forward_rows(1)
    forward_rows(3)
    for n in COLUMN_ORDER[1:]:
        forward_cols(n)
    wait_set(0)
    for copy in counts_in:
        copy.wait()
    wait_cols(0)
    wait_cols(3 - 2 * odd)
    tile_step(set_at(0), 2 * pair, 2 * TILE, True, True)
    wait_cols(2)
    wait_cols(1 + 2 * odd)
    forward_rows(2)
    tile_step(set_at(0), 2 - 2 * pair, 2 * TILE, False, True)
    encode_rows(0)

    for d in SETS[:2]:
        wait_set(d)
        for tile in (0, 2):
            tile_step(set_at(d), tile, 2 * TILE, tile == 0, False)
        encode_rows(d)
        send_rows(d)
        if d == SETS[0]:
            send_rows(0)

    def core_message(n):
        return remote(c_out.at[n], c_in.at[n], rc_send.at[n], rc_recv.at[n], row_peer(0, 0, 1))

    def x_message(n):
        return remote(x_out.at[n], x_in.at[n], rx_send.at[n], rx_recv.at[n], row_peer(n + 1, 0, 0))

    def core_rows(n, h, core):
        return part_at(lax.rem(x + 1 + n, 4) * 4 + 2 * h + core)

    def send_core(n):
        theirs = [col_total[core_rows(n, h, 1 - c), :] for h in (0, 1)]
        encode(c_out.at[n], jnp.concatenate(theirs, axis=0))
        core_message(n).start()

    wait_set(SETS[2])
    tile_step(set_at(SETS[2]), 2 - 2 * pair, 2 * TILE, True, False)
    send_core(1)
    send_core(2 - 2 * odd)
    tile_step(set_at(SETS[2]), 2 * pair, 2 * TILE, False, False)
    encode_rows(SETS[2])
    send_rows(SETS[2])
    send_core(2 * odd)
    send_core(3)
    send_z(SETS[0])

    def both_cores(n):
        core_message(n).wait_recv()
        mine = [col_total[core_rows(n, h, c), :] for h in (0, 1)]
        return decode(c_in.at[n], 2 * PART) + jnp.concatenate(mine, axis=0)

    for n in (1, 2 - 2 * odd, 2 * odd):
        encode(x_out.at[n], both_cores(n))
        x_message(n).start()
    both = both_cores(3)

    send_z(SETS[1])
    send_far()
    send_z(SETS[2])
    for n in range(3):
        x_message(n).wait_recv()
        both = both + decode(x_in.at[n], 2 * PART)
    here = jnp.where(zl == 0, both[0:PART], both[PART:])
    encode(l_out, jnp.where(zl == 0, both[PART:], both[0:PART]))
    l_message = go(remote(l_out, l_in, rl_send, rl_recv, row_peer(0, 1, 0)))
    row_sum = sum_rows(0)

    for copy in sends:
        copy.wait_send()
    for d in (0, 1, 2, 3):
        for e in (1, 3) if d % 2 else (1, 2, 3):
            y_message(d, e).wait_send()
    for d in (1, 3):
        far_message(d).wait_send()
    for n in range(4):
        core_message(n).wait_send()
    for n in range(3):
        x_message(n).wait_send()
    l_message.wait_recv()
    col_out[...] = here + decode(l_in, PART)
    for d in SETS:
        z_message(d).wait_recv()
        row_sum = row_sum + decode(z_in.at[d - 1], CHUNK)
    row_out[...] = row_sum
    for d in SETS:
        z_message(d).wait_send()


def shards(counts, row_sums, col_sums, log_total, row_emb, col_emb):
    n_cols = lax.axis_size("cols")
    scale = 1.0 / math.sqrt(col_sums.shape[0] * n_cols)
    dma = pltpu.SemaphoreType.DMA

    def body(*refs):
        kernel(scale, *refs)

    def hbm(array):
        return pltpu.with_memory_space_constraint(array, pltpu.HBM)

    anywhere = pl.BlockSpec(memory_space=pl.ANY)
    vmem = pl.BlockSpec(memory_space=pltpu.VMEM)
    message = (CHUNK + 16, D)
    return pl.pallas_call(
        body,
        name="swivel",
        out_shape=(
            jax.ShapeDtypeStruct((CHUNK, D), jnp.float32),
            jax.ShapeDtypeStruct((PART, D), jnp.float32),
        ),
        in_specs=[anywhere] * 3 + [pl.BlockSpec(memory_space=pltpu.SMEM)] + [anywhere] * 2,
        out_specs=(vmem, vmem),
        scratch_shapes=[
            pltpu.VMEM(counts.shape, jnp.int32),
            pltpu.VMEM((16, CHUNK), jnp.int32),
            pltpu.VMEM((8, CHUNK), jnp.int32),
            pltpu.VMEM((16 * CHUNK, D), jnp.bfloat16),
            pltpu.VMEM((16 * PART, D), jnp.bfloat16),
            pltpu.VMEM((16 * CHUNK, CHUNK), jnp.float32),
            pltpu.VMEM((4, 8, TILE), jnp.float32),
            pltpu.VMEM((4, CHUNK, D), jnp.float32),
            pltpu.VMEM((CHUNK, D), jnp.float32),
            pltpu.VMEM((SET, D), jnp.float32),
            pltpu.VMEM((16 * PART, D), jnp.float32),
            pltpu.VMEM((4, 3) + message, jnp.int16),
            pltpu.VMEM((4, 3) + message, jnp.int16),
            pltpu.VMEM((2,) + message, jnp.int16),
            pltpu.VMEM((3,) + message, jnp.int16),
            pltpu.VMEM((3,) + message, jnp.int16),
            pltpu.VMEM((4,) + message, jnp.int16),
            pltpu.VMEM((4,) + message, jnp.int16),
            pltpu.VMEM((3,) + message, jnp.int16),
            pltpu.VMEM((3,) + message, jnp.int16),
            pltpu.VMEM((PART + 16, D), jnp.int16),
            pltpu.VMEM((PART + 16, D), jnp.int16),
            dma((4,)),
            dma((4,)),
            dma((4,)), dma((4,)),
            dma((4, 4)), dma((4, 4)),
            dma((7,)), dma((7,)),
            dma((8,)), dma((8,)),
            dma((4, 4)), dma((4, 4)),
            dma((2,)), dma((2,)),
            dma((4,)), dma((4,)),
            dma((4,)), dma((4,)),
            dma((3,)), dma((3,)),
            dma, dma,
        ],
        compiler_params=pltpu.CompilerParams(
            collective_id=0, has_side_effects=True, vmem_limit_bytes=48 << 20
        ),
        cost_estimate=pl.CostEstimate(
            flops=6 * 2048 * 1024 * 256, bytes_accessed=9 << 20, transcendentals=3 * 2048 * 1024
        ),
    )(
        counts, hbm(row_sums.reshape(16, CHUNK)), hbm(col_sums.reshape(8, CHUNK)), log_total, hbm(row_emb), hbm(col_emb)
    )


def solution(mesh):
    in_specs = (
        P("rows", "cols"),
        P("rows"),
        P("cols"),
        P(),
        P(("rows", "cols"), None),
        P(("cols", "rows"), None),
    )
    out_specs = (P(("rows", "cols"), None), P(("cols", "rows"), None))
    return jax.shard_map(shards, mesh=mesh, in_specs=in_specs, out_specs=out_specs, check_vma=False)
```

time: 52.7 us -> 46.5 us (0.88)
  the two profiles are of different devices: /device:TPU:1 before, /device:TPU:33 now
where the time goes in v2:
time: 46.5 us; the launch traced here: 46.4 us
  Pallas kernels  43.8 us (94%)
  local copies, waits for them, and re-layouts  1.29 us (3%)
  between operations  1.29 us (3%)
    pallas_call x1, Pallas kernels, shards(): pl.pallas_call(body, name='swivel', out_shape=(jax.ShapeDtypeStruct((CHUN...  43.8 us
    unnamed x2, local copies, waits for them, and re-layouts  1.29 us

profile of v2, /device:TPU:33, one launch (start us, length us, event | category | flops | bytes accessed | tf_op | source)
XLA Modules:
  0.0 46.4 jit_solution(16584078443786282859)
XLA Ops:
  1.3 43.8 %swivel.1 = (f32[128,256]{1,0:T(8,128)S(1)}, f32[64,256]{1,0:T(8,128)S(1)}) custom-call(s32[2048,1024]{1,0:T(8,128)} %refs_0_.1, s32[16,128]{1,0:T(8,128)} %bitcast.2, s32[8,128]{1,0:T(8,128)} %bitcast.3, f32[1]{0:T(128)S(6)} %copy.10.refs_3_, bf16[128,256]{1,0:T(8,128)(2,1)} %refs_4_.1, bf16[64,256]{1,0:T(8,128)(2,1)} %refs_5_.1), custom_call_target="tpu_custom_call" | custom-call | flops 3221225472 | bytes 9437184 | tf_op jit(solution)/shard_map/swivel/pallas_call | solution.py:355
  45.1 0.7 %copy.11 = f32[128,256]{1,0:T(8,128)} copy(f32[128,256]{1,0:T(8,128)S(1)} %get-tuple-element.4) | data formatting | bytes 262144
  45.8 0.6 %copy.12 = f32[64,256]{1,0:T(8,128)} copy(f32[64,256]{1,0:T(8,128)S(1)} %get-tuple-element.5) | data formatting | bytes 131072

commit v3 on v2

--- a/solution.py
+++ b/solution.py
@@ -16,7 +16,7 @@
 LEVELS = 32000.0
 STEPS = 8.0
 COLUMN_ORDER = (0, 1, 5, 3, 2, 6, 4)
-SETS = (1, 2, 3)
+SETS = (1, 3, 2)
 
 
 def encode(ref, value):
@@ -52,9 +52,9 @@
     counts, row_sums, col_sums, rows, cols, row_bias, col_bias,
     kept, far, row_total, col_total,
     y_out, y_in, b_in, z_out, z_in, c_out, c_in, x_out, x_in, l_out, l_in,
-    local_sem, counts_sem,
-    gz_send, gz_recv, gy_send, gy_recv, gx_send, gx_recv, gc_send, gc_recv,
-    ry_send, ry_recv, rb_send, rb_recv, rz_send, rz_recv, rc_send, rc_recv, rx_send, rx_recv, rl_send, rl_recv,
+    local_sem, counts_sem, sent,
+    gz_recv, gs_recv, gf_recv, gx_recv, gc_recv,
+    ry_recv, rb_recv, rz_recv, rc_recv, rx_recv, rl_recv,
 ):
     r, k = lax.axis_index("rows"), lax.axis_index("cols")
     x, zl, c = r // 4, (r // 2) % 2, r % 2
@@ -96,39 +96,40 @@
     counts_in = []
     for n in range(4):
         at = pl.ds(n * SET, SET)
-        counts_in.append(pltpu.make_async_copy(counts_hbm.at[at], counts.at[at], counts_sem.at[n]))
+        counts_in.append(pltpu.make_async_copy(counts_hbm.at[at], counts.at[at], counts_sem))
         counts_in[-1].start()
     for copy in local:
         copy.wait()
     pl.semaphore_wait(barrier, len(peers))
 
-    sends = []
-
-    def go(copy):
-        copy.start()
-        sends.append(copy)
-        return copy
-
-    def z_gather(d):
-        at = chunk_at(lax.rem(zh + 4 - d, 4), y)
-        return remote(rows.at[at], rows.at[at], gz_send.at[d], gz_recv.at[d], col_peer(d, 0))
+    def give_rows(at, recv, to):
+        remote(rows.at[at], rows.at[at], sent.at[0], recv, to).start()
+
+    def give_cols(at, recv, to):
+        remote(cols.at[at], cols.at[at], sent.at[1], recv, to).start()
+
+    def wait_rows(count, recv):
+        at = pl.ds(0, count)
+        remote(rows.at[at], rows.at[at], sent.at[0], recv, col_peer(0, 1)).wait_recv()
+
+    def wait_parts(count, recv):
+        at = pl.ds(0, count * PART)
+        remote(cols.at[at], cols.at[at], sent.at[1], recv, row_peer(0, 0, 1)).wait_recv()
 
     def send_cols(dx, dl):
-        at, n = part_at(x * 4 + lax.rem(zl + dl, 2) * 2 + c), 2 * dx + dl - 1
-        go(remote(cols.at[at], cols.at[at], gx_send.at[n], gx_recv.at[n], row_peer(dx, 0, 0)))
-
-    def send_own_rows(d):
-        go(remote(rows.at[own_rows], rows.at[own_rows], gz_send.at[d], gz_recv.at[d], col_peer(d, 0)))
-
-    send_own_rows(1)
-    send_own_rows(3)
-    go(remote(cols.at[own_cols], cols.at[own_cols], gc_send.at[7], gc_recv.at[7], row_peer(0, 0, 1)))
-    go(remote(cols.at[own_cols], cols.at[own_cols], gx_send.at[0], gx_recv.at[0], row_peer(0, 1, 0)))
+        at = part_at(x * 4 + lax.rem(zl + dl, 2) * 2 + c)
+        give_cols(at, gx_recv.at[2 * dx + dl - 1], row_peer(dx, 0, 0))
+
+    give_cols(own_cols, gx_recv.at[0], row_peer(0, 1, 0))
+    give_rows(own_rows, gz_recv.at[1], col_peer(1, 0))
+    give_rows(own_rows, gz_recv.at[3], col_peer(3, 0))
+    give_rows(own_rows, gf_recv, col_peer(0, 2))
+    give_rows(own_rows, gs_recv.at[0], col_peer(0, 1))
+    give_rows(own_rows, gs_recv.at[0], col_peer(0, 3))
+    give_cols(own_cols, gc_recv.at[0], row_peer(0, 0, 1))
     for dx in (1, 3, 2):
         send_cols(dx, 0)
-    for e in (1, 3, 2):
-        go(remote(rows.at[own_rows], rows.at[own_rows], gy_send.at[0, e], gy_recv.at[0, e], col_peer(0, e)))
-    send_own_rows(2)
+    give_rows(own_rows, gz_recv.at[2], col_peer(2, 0))
 
     row_logs = jnp.log(row_sums[...].astype(jnp.float32)) - log_total[0]
     for n in range(16):
@@ -140,36 +141,29 @@
         col_bias[t] = jnp.concatenate(both, axis=1)
 
     def forward_rows(d):
-        at = chunk_at(lax.rem(zh + 4 - d, 4), y)
-        z_gather(d).wait_recv()
-        for e in (1, 3, 2):
-            go(remote(rows.at[at], rows.at[at], gy_send.at[d, e], gy_recv.at[d, e], col_peer(0, e)))
-
-    def y_gather(d, e):
-        at = chunk_at(lax.rem(zh + 4 - d, 4), lax.rem(y + 4 - e, 4))
-        return remote(rows.at[at], rows.at[at], gy_send.at[d, e], gy_recv.at[d, e], col_peer(0, e))
-
-    def origin(dx, dl, core):
-        return part_at(lax.rem(x + 4 - dx, 4) * 4 + lax.rem(zl + dl, 2) * 2 + core)
+        wait_rows(CHUNK, gz_recv.at[d])
+        for e in (1, 3) if d % 2 else (2, 1, 3):
+            give_rows(chunk_at(lax.rem(zh + 4 - d, 4), y), gs_recv.at[d], col_peer(0, e))
+
+    def forward_far():
+        wait_rows(CHUNK, gf_recv)
+        for d in (1, 3):
+            give_rows(chunk_at(zh, lax.rem(y + 2, 4)), gs_recv.at[d], col_peer(d, 0))
 
     def forward_cols(n):
         dx, dl = same_core[n]
-        at = origin(dx, dl, c)
-        remote(cols.at[at], cols.at[at], gx_send.at[n], gx_recv.at[n], row_peer(dx, dl, 0)).wait_recv()
-        go(remote(cols.at[at], cols.at[at], gc_send.at[n], gc_recv.at[n], row_peer(0, 0, 1)))
+        wait_parts(1, gx_recv.at[n])
+        at = part_at(lax.rem(x + 4 - dx, 4) * 4 + lax.rem(zl + dl, 2) * 2 + c)
+        give_cols(at, gc_recv.at[dx], row_peer(0, 0, 1))
         if n == 0:
             for peer in (1, 3, 2):
                 send_cols(peer, 1)
 
     def wait_cols(dx):
-        for dl in (0, 1):
-            n = lax.rem(2 * dx + dl + 7, 8)
-            at = origin(dx, dl, 1 - c)
-            remote(cols.at[at], cols.at[at], gc_send.at[n], gc_recv.at[n], row_peer(0, 0, 1)).wait_recv()
+        wait_parts(2, gc_recv.at[dx])
 
     def wait_set(d):
-        for e in (1, 3, 2):
-            y_gather(d, e).wait_recv()
+        wait_rows((3 if d else 2) * CHUNK, gs_recv.at[d])
 
     def grads_of(at, tile, width):
         col_at = pl.ds(pl.multiple_of(tile * TILE, TILE), width)
@@ -193,17 +187,17 @@
     def set_at(d):
         return pl.ds(pl.multiple_of(lax.rem(zh + 4 - d, 4) * SET, SET), SET)
 
+    slot_of = {1: 0, 3: 1, 2: 2}
+
     def y_message(d, e):
-        return remote(
-            y_out.at[d, e - 1], y_in.at[d, e - 1], ry_send.at[d, e], ry_recv.at[d, e], col_peer(0, e)
-        )
+        n = slot_of[e]
+        return remote(y_out.at[d, n], y_in.at[d, n], sent.at[2], ry_recv.at[d], col_peer(0, e))
 
     def far_message(d):
-        n = d // 2
-        return remote(y_out.at[d, 1], b_in.at[n], rb_send.at[n], rb_recv.at[n], col_peer(4 - d, 0))
+        return remote(y_out.at[d, 2], b_in.at[d // 2], sent.at[2], rb_recv, col_peer(4 - d, 0))
 
     def z_message(d):
-        return remote(z_out.at[d - 1], z_in.at[d - 1], rz_send.at[d], rz_recv.at[d], col_peer(4 - d, 0))
+        return remote(z_out.at[d - 1], z_in.at[d - 1], sent.at[3], rz_recv, col_peer(4 - d, 0))
 
     def peer_rows(e):
         return row_total[pl.ds(pl.multiple_of(lax.rem(y + e, 4) * CHUNK, CHUNK), CHUNK), :]
@@ -212,9 +206,9 @@
         if d == 0:
             far[...] = peer_rows(2)
         else:
-            encode(y_out.at[d, 1], peer_rows(2))
+            encode(y_out.at[d, 2], peer_rows(2))
         encode(y_out.at[d, 0], peer_rows(1))
-        encode(y_out.at[d, 2], peer_rows(3))
+        encode(y_out.at[d, 1], peer_rows(3))
         kept[d] = peer_rows(0)
 
     def send_rows(d):
@@ -226,18 +220,17 @@
         y_message(d, 3).start()
 
     def send_far():
-        for d in (1, 3):
-            far_message(d).wait_recv()
-        encode(y_out.at[0, 1], far[...] + decode(b_in.at[0], CHUNK) + decode(b_in.at[1], CHUNK))
+        remote(b_in, b_in, sent.at[2], rb_recv, col_peer(1, 0)).wait_recv()
+        encode(y_out.at[0, 2], far[...] + decode(b_in.at[0], CHUNK) + decode(b_in.at[1], CHUNK))
         y_message(0, 2).start()
 
     def sum_rows(d):
-        hops = (1, 3) if d % 2 else (1, 3, 2)
+        hops = 2 if d % 2 else 3
+        arrived = y_in.at[d, pl.ds(0, hops)]
+        remote(arrived, arrived, sent.at[2], ry_recv.at[d], col_peer(0, 1)).wait_recv()
         total = kept[d]
-        for e in hops:
-            y_message(d, e).wait_recv()
-        for e in hops:
-            total = total + decode(y_in.at[d, e - 1], CHUNK)
+        for n in range(hops):
+            total = total + decode(y_in.at[d, n], CHUNK)
         return total
 
     def send_z(d):
@@ -248,17 +241,20 @@
     forward_cols(0)
     forward_rows(1)
     forward_rows(3)
-    for n in COLUMN_ORDER[1:]:
+    forward_far()
+    for n in COLUMN_ORDER[1:4]:
         forward_cols(n)
     wait_set(0)
-    for copy in counts_in:
-        copy.wait()
+    pltpu.make_async_copy(counts_hbm, counts, counts_sem).wait()
     wait_cols(0)
+    tile_step(set_at(0), x, TILE, True, True)
+    for n in COLUMN_ORDER[4:]:
+        forward_cols(n)
     wait_cols(3 - 2 * odd)
-    tile_step(set_at(0), 2 * pair, 2 * TILE, True, True)
+    tile_step(set_at(0), 2 * pair + 1 - odd, TILE, False, True)
+    forward_rows(2)
     wait_cols(2)
     wait_cols(1 + 2 * odd)
-    forward_rows(2)
     tile_step(set_at(0), 2 - 2 * pair, 2 * TILE, False, True)
     encode_rows(0)
 
@@ -272,10 +268,10 @@
             send_rows(0)
 
     def core_message(n):
-        return remote(c_out.at[n], c_in.at[n], rc_send.at[n], rc_recv.at[n], row_peer(0, 0, 1))
+        return remote(c_out.at[n], c_in.at[n], sent.at[4], rc_recv.at[n], row_peer(0, 0, 1))
 
     def x_message(n):
-        return remote(x_out.at[n], x_in.at[n], rx_send.at[n], rx_recv.at[n], row_peer(n + 1, 0, 0))
+        return remote(x_out.at[n], x_in.at[n], sent.at[5], rx_recv, row_peer(n + 1, 0, 0))
 
     def core_rows(n, h, core):
         return part_at(lax.rem(x + 1 + n, 4) * 4 + 2 * h + core)
@@ -307,35 +303,28 @@
     both = both_cores(3)
 
     send_z(SETS[1])
+    send_z(SETS[2])
     send_far()
-    send_z(SETS[2])
+    remote(x_in, x_in, sent.at[5], rx_recv, row_peer(1, 0, 0)).wait_recv()
     for n in range(3):
-        x_message(n).wait_recv()
         both = both + decode(x_in.at[n], 2 * PART)
     here = jnp.where(zl == 0, both[0:PART], both[PART:])
     encode(l_out, jnp.where(zl == 0, both[PART:], both[0:PART]))
-    l_message = go(remote(l_out, l_in, rl_send, rl_recv, row_peer(0, 1, 0)))
+    l_message = remote(l_out, l_in, sent.at[6], rl_recv, row_peer(0, 1, 0))
+    l_message.start()
     row_sum = sum_rows(0)
-
-    for copy in sends:
-        copy.wait_send()
-    for d in (0, 1, 2, 3):
-        for e in (1, 3) if d % 2 else (1, 2, 3):
-            y_message(d, e).wait_send()
-    for d in (1, 3):
-        far_message(d).wait_send()
-    for n in range(4):
-        core_message(n).wait_send()
-    for n in range(3):
-        x_message(n).wait_send()
     l_message.wait_recv()
     col_out[...] = here + decode(l_in, PART)
+
+    for n, ref in (
+        (0, rows.at[pl.ds(0, 15 * CHUNK)]), (1, cols.at[pl.ds(0, 15 * PART)]),
+        (2, y_out), (3, z_out), (4, c_out), (5, x_out), (6, l_out),
+    ):
+        remote(ref, ref, sent.at[n], rl_recv, col_peer(0, 1)).wait_send()
+    remote(z_in, z_in, sent.at[3], rz_recv, col_peer(1, 0)).wait_recv()
     for d in SETS:
-        z_message(d).wait_recv()
         row_sum = row_sum + decode(z_in.at[d - 1], CHUNK)
     row_out[...] = row_sum
-    for d in SETS:
-        z_message(d).wait_send()
 
 
 def shards(counts, row_sums, col_sums, log_total, row_emb, col_emb):
@@ -384,18 +373,9 @@
             pltpu.VMEM((3,) + message, jnp.int16),
             pltpu.VMEM((PART + 16, D), jnp.int16),
             pltpu.VMEM((PART + 16, D), jnp.int16),
-            dma((4,)),
-            dma((4,)),
-            dma((4,)), dma((4,)),
-            dma((4, 4)), dma((4, 4)),
-            dma((7,)), dma((7,)),
-            dma((8,)), dma((8,)),
-            dma((4, 4)), dma((4, 4)),
-            dma((2,)), dma((2,)),
-            dma((4,)), dma((4,)),
-            dma((4,)), dma((4,)),
-            dma((3,)), dma((3,)),
-            dma, dma,
+            dma((4,)), dma, dma((7,)),
+            dma((4,)), dma((4,)), dma, dma((7,)), dma((4,)),
+            dma((4,)), dma, dma, dma((4,)), dma, dma,
         ],
         compiler_params=pltpu.CompilerParams(
             collective_id=0, has_side_effects=True, vmem_limit_bytes=48 << 20

time: 46.5 us -> 43.2 us (0.929)
  the two profiles are of different devices: /device:TPU:33 before, /device:TPU:1 now
where the time goes in v3:
time: 43.2 us; the launch traced here: 42.6 us
  Pallas kernels  40.1 us (93%)
  local copies, waits for them, and re-layouts  1.29 us (3%)
  between operations  1.29 us (3%)
    pallas_call x1, Pallas kernels, shards(): pl.pallas_call(body, name='swivel', out_shape=(jax.ShapeDtypeStruct((CHUN...  40.1 us
    unnamed x2, local copies, waits for them, and re-layouts  1.29 us

profile of v3, /device:TPU:1, one launch (start us, length us, event | category | flops | bytes accessed | tf_op | source)
XLA Modules:
  0.0 42.6 jit_solution(225227953733131067)
XLA Ops:
  1.3 40.1 %swivel.1 = (f32[128,256]{1,0:T(8,128)S(1)}, f32[64,256]{1,0:T(8,128)S(1)}) custom-call(s32[2048,1024]{1,0:T(8,128)} %refs_0_.1, s32[16,128]{1,0:T(8,128)} %bitcast.2, s32[8,128]{1,0:T(8,128)} %bitcast.3, f32[1]{0:T(128)S(6)} %copy.10.refs_3_, bf16[128,256]{1,0:T(8,128)(2,1)} %refs_4_.1, bf16[64,256]{1,0:T(8,128)(2,1)} %refs_5_.1), custom_call_target="tpu_custom_call" | custom-call | flops 3221225472 | bytes 9437184 | tf_op jit(solution)/shard_map/swivel/pallas_call | solution.py:344
  41.3 0.7 %copy.11 = f32[128,256]{1,0:T(8,128)} copy(f32[128,256]{1,0:T(8,128)S(1)} %get-tuple-element.4) | data formatting | bytes 262144
  42.0 0.6 %copy.12 = f32[64,256]{1,0:T(8,128)} copy(f32[64,256]{1,0:T(8,128)S(1)} %get-tuple-element.5) | data formatting | bytes 131072

commit v4 on v3

--- a/solution.py
+++ b/solution.py
@@ -184,6 +184,23 @@
         )
         col_total[col_at, :] = part if first_cols else col_total[col_at, :] + part
 
+    def half_step(d, hops):
+        z = lax.rem(zh + 4 - d, 4)
+        ats = [chunk_at(z, lax.rem(y + e, 4)) for e in hops]
+        some = jnp.concatenate([rows[at, :] for at in ats], axis=0)
+        scores = lax.dot_general(
+            some, cols[...], (((1,), (1,)), ((), ())), preferred_element_type=jnp.float32
+        )
+        bias = jnp.concatenate([row_bias[at, :] for at in ats], axis=0)
+        bias = jnp.concatenate([bias] * (4 * TILE // CHUNK), axis=1)
+        side = jnp.concatenate([col_bias[n, 0:1, :] for n in range(4)], axis=1)
+        found = jnp.concatenate([counts[at, :] for at in ats], axis=0)
+        grads = cell_grads(found, scores + bias + side, scale)
+        col_total[...] += lax.dot_general(
+            grads, some, (((0,), (0,)), ((), ())), preferred_element_type=jnp.float32
+        )
+        return jnp.dot(grads, cols[...], preferred_element_type=jnp.float32)
+
     def set_at(d):
         return pl.ds(pl.multiple_of(lax.rem(zh + 4 - d, 4) * SET, SET), SET)
 
@@ -239,17 +256,17 @@
 
     odd, pair = x % 2, x // 2
     forward_cols(0)
+    for n in COLUMN_ORDER[1:4]:
+        forward_cols(n)
     forward_rows(1)
     forward_rows(3)
     forward_far()
-    for n in COLUMN_ORDER[1:4]:
-        forward_cols(n)
     wait_set(0)
     pltpu.make_async_copy(counts_hbm, counts, counts_sem).wait()
     wait_cols(0)
-    tile_step(set_at(0), x, TILE, True, True)
     for n in COLUMN_ORDER[4:]:
         forward_cols(n)
+    tile_step(set_at(0), x, TILE, True, True)
     wait_cols(3 - 2 * odd)
     tile_step(set_at(0), 2 * pair + 1 - odd, TILE, False, True)
     forward_rows(2)
@@ -264,8 +281,6 @@
             tile_step(set_at(d), tile, 2 * TILE, tile == 0, False)
         encode_rows(d)
         send_rows(d)
-        if d == SETS[0]:
-            send_rows(0)
 
     def core_message(n):
         return remote(c_out.at[n], c_in.at[n], sent.at[4], rc_recv.at[n], row_peer(0, 0, 1))
@@ -281,15 +296,19 @@
         encode(c_out.at[n], jnp.concatenate(theirs, axis=0))
         core_message(n).start()
 
-    wait_set(SETS[2])
-    tile_step(set_at(SETS[2]), 2 - 2 * pair, 2 * TILE, True, False)
-    send_core(1)
-    send_core(2 - 2 * odd)
-    tile_step(set_at(SETS[2]), 2 * pair, 2 * TILE, False, False)
-    encode_rows(SETS[2])
-    send_rows(SETS[2])
-    send_core(2 * odd)
-    send_core(3)
+    wait_set(2)
+    row_part = half_step(2, (2, 1))
+    encode(y_out.at[2, 2], row_part[0:CHUNK])
+    encode(y_out.at[2, 0], row_part[CHUNK:])
+    y_message(2, 2).start()
+    y_message(2, 1).start()
+    row_part = half_step(2, (3, 0))
+    encode(y_out.at[2, 1], row_part[0:CHUNK])
+    y_message(2, 3).start()
+    kept[2] = row_part[CHUNK:]
+    for n in (1, 2 - 2 * odd, 2 * odd, 3):
+        send_core(n)
+    send_rows(0)
     send_z(SETS[0])
 
     def both_cores(n):
@@ -303,8 +322,8 @@
     both = both_cores(3)
 
     send_z(SETS[1])
+    send_far()
     send_z(SETS[2])
-    send_far()
     remote(x_in, x_in, sent.at[5], rx_recv, row_peer(1, 0, 0)).wait_recv()
     for n in range(3):
         both = both + decode(x_in.at[n], 2 * PART)

time: 43.2 us -> 41.8 us (0.968)
  Pallas kernels: 40.1 us -> 39.1 us
    pallas_call x1, Pallas kernels: 40.1 us -> 39.1 us  [shards(): pl.pallas_call(body, name='swivel', out_shape=(jax.ShapeDtypeStruct((CHUN...]
where the time goes in v4:
time: 41.8 us; the launch traced here: 41.7 us
  Pallas kernels  39.1 us (94%)
  local copies, waits for them, and re-layouts  1.29 us (3%)
  between operations  1.29 us (3%)
    pallas_call x1, Pallas kernels, shards(): pl.pallas_call(body, name='swivel', out_shape=(jax.ShapeDtypeStruct((CHUN...  39.1 us
    unnamed x2, local copies, waits for them, and re-layouts  1.29 us

profile of v4, /device:TPU:1, one launch (start us, length us, event | category | flops | bytes accessed | tf_op | source)
XLA Modules:
  0.0 41.7 jit_solution(18125640354516250575)
XLA Ops:
  1.3 39.1 %swivel.1 = (f32[128,256]{1,0:T(8,128)S(1)}, f32[64,256]{1,0:T(8,128)S(1)}) custom-call(s32[2048,1024]{1,0:T(8,128)} %refs_0_.1, s32[16,128]{1,0:T(8,128)} %bitcast.2, s32[8,128]{1,0:T(8,128)} %bitcast.3, f32[1]{0:T(128)S(6)} %copy.10.refs_3_, bf16[128,256]{1,0:T(8,128)(2,1)} %refs_4_.1, bf16[64,256]{1,0:T(8,128)(2,1)} %refs_5_.1), custom_call_target="tpu_custom_call" | custom-call | flops 3221225472 | bytes 9437184 | tf_op jit(solution)/shard_map/swivel/pallas_call | solution.py:363
  40.4 0.7 %copy.11 = f32[128,256]{1,0:T(8,128)} copy(f32[128,256]{1,0:T(8,128)S(1)} %get-tuple-element.4) | data formatting | bytes 262144
  41.0 0.6 %copy.12 = f32[64,256]{1,0:T(8,128)} copy(f32[64,256]{1,0:T(8,128)S(1)} %get-tuple-element.5) | data formatting | bytes 131072

commit v5 on v4

--- a/solution.py
+++ b/solution.py
@@ -36,20 +36,24 @@
     return ref[0:rows, :].astype(jnp.int32).astype(jnp.float32) * scale
 
 
-def cell_grads(counts, scores, scale):
+def of_counts(counts, scale):
     at_least_one = jnp.maximum(counts.astype(jnp.float32), 1.0)
     root = at_least_one * lax.rsqrt(at_least_one)
     conf = (0.1 * scale) + (0.25 * scale) * root
-    fitted = conf * (scores - jnp.log(at_least_one))
+    return jnp.where(counts > 0, conf, -1.0), conf * jnp.log(at_least_one)
+
+
+def cell_grads(conf, logs, scores, scale):
+    fitted = conf * scores - logs
     hinge = (0.5 * scale) + (0.5 * scale) * jnp.tanh(0.5 * scores)
-    return jnp.where(counts > 0, fitted, hinge).astype(jnp.bfloat16)
+    return jnp.where(conf > 0, fitted, hinge).astype(jnp.bfloat16)
 
 
 def kernel(
     scale,
     counts_hbm, row_sums_hbm, col_sums_hbm, log_total, row_emb, col_emb,
     row_out, col_out,
-    counts, row_sums, col_sums, rows, cols, row_bias, col_bias,
+    counts, confs, count_logs, row_sums, col_sums, rows, cols, row_bias, col_bias,
     kept, far, row_total, col_total,
     y_out, y_in, b_in, z_out, z_in, c_out, c_in, x_out, x_in, l_out, l_in,
     local_sem, counts_sem, sent,
@@ -140,6 +144,15 @@
         both = [jnp.broadcast_to(col_logs[2 * t + h : 2 * t + h + 1, :], (8, CHUNK)) for h in (0, 1)]
         col_bias[t] = jnp.concatenate(both, axis=1)
 
+    pltpu.make_async_copy(counts_hbm, counts, counts_sem).wait()
+
+    def prepare(step, _):
+        at = pl.ds(pl.multiple_of(lax.rem(zh * 4 + 4 + step, 16) * CHUNK, CHUNK), CHUNK)
+        confs[at, :], count_logs[at, :] = of_counts(counts[at, :], scale)
+        return 0
+
+    lax.fori_loop(0, 12, prepare, 0)
+
     def forward_rows(d):
         wait_rows(CHUNK, gz_recv.at[d])
         for e in (1, 3) if d % 2 else (2, 1, 3):
@@ -165,7 +178,7 @@
     def wait_set(d):
         wait_rows((3 if d else 2) * CHUNK, gs_recv.at[d])
 
-    def grads_of(at, tile, width):
+    def grads_of(at, tile, width, own):
         col_at = pl.ds(pl.multiple_of(tile * TILE, TILE), width)
         some = cols[col_at, :]
         scores = lax.dot_general(
@@ -173,10 +186,14 @@
         )
         bias = jnp.concatenate([row_bias[at, :]] * (width // CHUNK), axis=1)
         side = jnp.concatenate([col_bias[tile + n, 0:1, :] for n in range(width // TILE)], axis=1)
-        return cell_grads(counts[at, col_at], scores + bias + side, scale), some, col_at
+        if own:
+            conf, logs = of_counts(counts[at, col_at], scale)
+        else:
+            conf, logs = confs[at, col_at], count_logs[at, col_at]
+        return cell_grads(conf, logs, scores + bias + side, scale), some, col_at
 
     def tile_step(at, tile, width, first_rows, first_cols):
-        grads, some, col_at = grads_of(at, tile, width)
+        grads, some, col_at = grads_of(at, tile, width, first_cols)
         part = jnp.dot(grads, some, preferred_element_type=jnp.float32)
         row_total[...] = part if first_rows else row_total[...] + part
         part = lax.dot_general(
@@ -194,8 +211,9 @@
         bias = jnp.concatenate([row_bias[at, :] for at in ats], axis=0)
         bias = jnp.concatenate([bias] * (4 * TILE // CHUNK), axis=1)
         side = jnp.concatenate([col_bias[n, 0:1, :] for n in range(4)], axis=1)
-        found = jnp.concatenate([counts[at, :] for at in ats], axis=0)
-        grads = cell_grads(found, scores + bias + side, scale)
+        conf = jnp.concatenate([confs[at, :] for at in ats], axis=0)
+        logs = jnp.concatenate([count_logs[at, :] for at in ats], axis=0)
+        grads = cell_grads(conf, logs, scores + bias + side, scale)
         col_total[...] += lax.dot_general(
             grads, some, (((0,), (0,)), ((), ())), preferred_element_type=jnp.float32
         )
@@ -262,7 +280,6 @@
     forward_rows(3)
     forward_far()
     wait_set(0)
-    pltpu.make_async_copy(counts_hbm, counts, counts_sem).wait()
     wait_cols(0)
     for n in COLUMN_ORDER[4:]:
         forward_cols(n)
@@ -371,6 +388,8 @@
         out_specs=(vmem, vmem),
         scratch_shapes=[
             pltpu.VMEM(counts.shape, jnp.int32),
+            pltpu.VMEM(counts.shape, jnp.float32),
+            pltpu.VMEM(counts.shape, jnp.float32),
             pltpu.VMEM((16, CHUNK), jnp.int32),
             pltpu.VMEM((8, CHUNK), jnp.int32),
             pltpu.VMEM((16 * CHUNK, D), jnp.bfloat16),

time: 41.8 us -> 40.9 us (0.978)
  Pallas kernels: 39.1 us -> 38.2 us
    pallas_call x1, Pallas kernels: 39.1 us -> 38.2 us  [shards(): pl.pallas_call(body, name='swivel', out_shape=(jax.ShapeDtypeStruct((CHUN...]
where the time goes in v5:
time: 40.9 us; the launch traced here: 40.8 us
  Pallas kernels  38.2 us (93%)
  local copies, waits for them, and re-layouts  1.29 us (3%)
  between operations  1.29 us (3%)
    pallas_call x1, Pallas kernels, shards(): pl.pallas_call(body, name='swivel', out_shape=(jax.ShapeDtypeStruct((CHUN...  38.2 us
    unnamed x2, local copies, waits for them, and re-layouts  1.29 us

profile of v5, /device:TPU:1, one launch (start us, length us, event | category | flops | bytes accessed | tf_op | source)
XLA Modules:
  0.0 40.8 jit_solution(17689275419269393659)
XLA Ops:
  1.3 38.2 %swivel.1 = (f32[128,256]{1,0:T(8,128)S(1)}, f32[64,256]{1,0:T(8,128)S(1)}) custom-call(s32[2048,1024]{1,0:T(8,128)} %refs_0_.1, s32[16,128]{1,0:T(8,128)} %bitcast.2, s32[8,128]{1,0:T(8,128)} %bitcast.3, f32[1]{0:T(128)S(6)} %copy.10.refs_3_, bf16[128,256]{1,0:T(8,128)(2,1)} %refs_4_.1, bf16[64,256]{1,0:T(8,128)(2,1)} %refs_5_.1), custom_call_target="tpu_custom_call" | custom-call | flops 3221225472 | bytes 9437184 | tf_op jit(solution)/shard_map/swivel/pallas_call | solution.py:380
  39.5 0.7 %copy.11 = f32[128,256]{1,0:T(8,128)} copy(f32[128,256]{1,0:T(8,128)S(1)} %get-tuple-element.4) | data formatting | bytes 262144
  40.1 0.6 %copy.12 = f32[64,256]{1,0:T(8,128)} copy(f32[64,256]{1,0:T(8,128)S(1)} %get-tuple-element.5) | data formatting | bytes 131072

commit v6 on v5

--- a/solution.py
+++ b/solution.py
@@ -292,12 +292,21 @@
     tile_step(set_at(0), 2 - 2 * pair, 2 * TILE, False, True)
     encode_rows(0)
 
-    for d in SETS[:2]:
-        wait_set(d)
-        for tile in (0, 2):
-            tile_step(set_at(d), tile, 2 * TILE, tile == 0, False)
-        encode_rows(d)
-        send_rows(d)
+    wait_set(1)
+    for tile in (0, 2):
+        tile_step(set_at(1), tile, 2 * TILE, tile == 0, False)
+    encode_rows(1)
+    send_rows(1)
+    wait_set(3)
+    row_part = half_step(3, (2, 1))
+    encode(y_out.at[3, 2], row_part[0:CHUNK])
+    encode(y_out.at[3, 0], row_part[CHUNK:])
+    far_message(3).start()
+    y_message(3, 1).start()
+    row_part = half_step(3, (3, 0))
+    encode(y_out.at[3, 1], row_part[0:CHUNK])
+    y_message(3, 3).start()
+    kept[3] = row_part[CHUNK:]
 
     def core_message(n):
         return remote(c_out.at[n], c_in.at[n], sent.at[4], rc_recv.at[n], row_peer(0, 0, 1))
@@ -325,7 +334,6 @@
     kept[2] = row_part[CHUNK:]
     for n in (1, 2 - 2 * odd, 2 * odd, 3):
         send_core(n)
-    send_rows(0)
     send_z(SETS[0])
 
     def both_cores(n):
@@ -339,6 +347,7 @@
     both = both_cores(3)
 
     send_z(SETS[1])
+    send_rows(0)
     send_far()
     send_z(SETS[2])
     remote(x_in, x_in, sent.at[5], rx_recv, row_peer(1, 0, 0)).wait_recv()

time: 40.9 us -> 40.5 us (level)
  no operation moved by 1% of the time
where the time goes in v6:
time: 40.5 us; the launch traced here: 40.4 us
  Pallas kernels  37.8 us (93%)
  local copies, waits for them, and re-layouts  1.29 us (3%)
  between operations  1.29 us (3%)
    pallas_call x1, Pallas kernels, shards(): pl.pallas_call(body, name='swivel', out_shape=(jax.ShapeDtypeStruct((CHUN...  37.8 us
    unnamed x2, local copies, waits for them, and re-layouts  1.29 us

profile of v6, /device:TPU:1, one launch (start us, length us, event | category | flops | bytes accessed | tf_op | source)
XLA Modules:
  0.0 40.4 jit_solution(10308962649768844491)
XLA Ops:
  1.3 37.8 %swivel.1 = (f32[128,256]{1,0:T(8,128)S(1)}, f32[64,256]{1,0:T(8,128)S(1)}) custom-call(s32[2048,1024]{1,0:T(8,128)} %refs_0_.1, s32[16,128]{1,0:T(8,128)} %bitcast.2, s32[8,128]{1,0:T(8,128)} %bitcast.3, f32[1]{0:T(128)S(6)} %copy.10.refs_3_, bf16[128,256]{1,0:T(8,128)(2,1)} %refs_4_.1, bf16[64,256]{1,0:T(8,128)(2,1)} %refs_5_.1), custom_call_target="tpu_custom_call" | custom-call | flops 3221225472 | bytes 9437184 | tf_op jit(solution)/shard_map/swivel/pallas_call | solution.py:389
  39.1 0.7 %copy.11 = f32[128,256]{1,0:T(8,128)} copy(f32[128,256]{1,0:T(8,128)S(1)} %get-tuple-element.4) | data formatting | bytes 262144
  39.8 0.6 %copy.12 = f32[64,256]{1,0:T(8,128)} copy(f32[64,256]{1,0:T(8,128)S(1)} %get-tuple-element.5) | data formatting | bytes 131072
